TPU v7x, 32 devices: a whole 2x2x4 slice. The times are simulated.
32 devices in a mesh: mode: 8 (over z, y), mer: 4 (over x, core).
Axes of the slice: x: 2, y: 2, z: 4, core: 2. Of those that a mesh axis runs over, the one named last changes fastest.
Arguments:
- mode_cost: int32 [32], replicated, may hold values from 105 to 420, as said below
- iface_index: int32 [128], replicated, may hold values from 0 to 255, as said below
- basis: float32 [4, 2, 64, 128, 256], P(None, None, 'mode', 'mer'), as said below
- radial: float32 [2, 256, 256], replicated, as said below
- axial: float32 [2, 128, 32], P(None, 'mer'), as said below
- flow_coupling: float32 [4, 128, 256], P(None, 'mer'), may hold values from -8 to 8
- swirl: float32 [128, 256], P('mer'), may hold values from -6 to 6
- shift: float32 [2], replicated, may hold values from 0.2 to 0.8
Outputs:
- new_vector: float32 [2, 64, 128, 256], P(None, 'mode', 'mer')
- coeffs: float32 [2, 4], replicated
- norm: float32 [], replicated
Inputs may be any that keep to these rules, and one draw needn't show every extreme that they name: `mode_cost`: every group has 2 to 8 modes and one group has exactly 8; within a group all costs are equal. `iface_index`: distinct and increasing; the first is 0 and the last is 255. `basis`: entries of order one to some tens. `radial`: each matrix has a unit diagonal plus entries of order 1 / sqrt(256). `axial`: each block has a unit diagonal plus entries of order 1 / sqrt(32).
All inputs are finite; a program needn't handle non-finite values.
Results may differ from a plain program's by a relative error of at most 0.000075.
Values sent between devices are 32-bit elements; how exact they have to be, the bound alone decides.
A program may use at most 64 MiB of HBM per device.

v0:
```python
import jax
import jax.numpy as jnp
from jax import lax
from jax.sharding import PartitionSpec as P

QUOTA = 840


penalty = 1.0
schur_diag = 2.2
epsilon = 1e-06


def passed_along(block, axis, distance):
    devices = range(lax.axis_size(axis))
    route = [(i - distance, i) for i in devices if i - distance in devices]
    return lax.ppermute(block, axis, route)


def padded_2(shard, sides, width):
    for axis, dim in sides:
        size, length = (lax.axis_size(axis), shard.shape[dim])
        up = [(i, (i + 1) % size) for i in range(size - 1)]
        down = [(j, i) for i, j in up]
        last = lax.slice_in_dim(shard, length - width, length, axis=dim)
        leading = lax.slice_in_dim(shard, 0, width, axis=dim)
        before = lax.ppermute(last, axis, up)
        after = lax.ppermute(leading, axis, down)
        shard = jnp.concatenate([before, shard, after], axis=dim)
    return shard


def solve_interface(rhs):
    count = rhs.shape[0]
    places = jnp.arange(count)
    diagonal = jnp.full((count,), schur_diag, rhs.dtype)
    below = jnp.where(places > 0, -1.0, 0.0).astype(rhs.dtype)
    above = jnp.where(places < count - 1, -1.0, 0.0).astype(rhs.dtype)
    return lax.linalg.tridiagonal_solve(below, diagonal, above, rhs)


def body(mode_cost, iface_index, basis, radial, axial, flow_coupling, swirl, shift):
    highest = lax.Precision.HIGHEST
    my_group = lax.axis_index("mode")
    slots = basis.shape[2]
    points = basis.shape[3]
    width = basis.shape[4]
    krylov = basis.shape[0]
    modes = mode_cost.shape[0]
    prefix = jnp.cumsum(mode_cost) - mode_cost
    owner = prefix // QUOTA
    count = jnp.sum((owner == my_group).astype(jnp.int32))
    start = jnp.sum((owner < my_group).astype(jnp.int32))
    below_count = jnp.sum((owner == my_group - 1).astype(jnp.int32))
    places = jnp.arange(slots)
    active = (places < count).astype(jnp.float32)
    basis_live = basis * active[None, None, :, None, None]
    current = basis_live[krylov - 1]
    lower_all = passed_along(current, "mode", 1)
    upper_all = passed_along(current, "mode", -1)
    lower = lax.dynamic_slice_in_dim(lower_all, below_count - 2, 2, axis=1)
    upper = upper_all[:, :2]
    radial_term = jnp.einsum("csir,tr->csit", current, radial[0], precision=highest)
    axial_term = jnp.einsum("ij,csjr->csir", axial[0], current, precision=highest)
    padded = padded_2(current, (("mer", 2),), 1)
    link = jnp.zeros_like(current)
    link = link.at[:, :, 0].add(padded[:, :, 0])
    link = link.at[:, :, -1].add(padded[:, :, -1])
    image = radial_term + (axial_term + penalty * link)
    empty = jnp.zeros((2, 2, points, width), current.dtype)
    extended = jnp.concatenate([lower, current, empty], axis=1)
    extended = lax.dynamic_update_slice_in_dim(extended, upper, count + 2, axis=1)
    for which, offset in enumerate((-2, -1, 1, 2)):
        image = image + flow_coupling[which] * extended[:, 2 + offset : 2 + offset + slots]
    wave = (start + places).astype(jnp.float32) / modes
    rotation = wave[:, None, None] * swirl[None]
    image_re = image[0] - rotation * current[1]
    image_im = image[1] + rotation * current[0]
    shifted_re = image_re - (shift[0] * current[0] - shift[1] * current[1])
    shifted_im = image_im - (shift[0] * current[1] + shift[1] * current[0])
    shifted = jnp.stack([shifted_re, shifted_im])
    local = jnp.einsum("ij,csjr->csir", axial[1], shifted, precision=highest)
    local = jnp.einsum("csir,tr->csit", local, radial[1], precision=highest)
    select = (iface_index[None, :] == jnp.arange(width)[:, None]).astype(jnp.float32)
    top_trace = jnp.einsum("csr,rp->csp", local[:, :, -1], select, precision=highest)
    bottom_trace = jnp.einsum("csr,rp->csp", local[:, :, 0], select, precision=highest)
    traces = lax.all_gather(jnp.stack([top_trace, bottom_trace])[None], "mer", axis=0, tiled=True)
    jumps = traces[:-1, 0] - traces[1:, 1]
    subdomains = lax.axis_size("mer")
    solved = solve_interface(jumps.reshape(subdomains - 1, -1)).reshape(jumps.shape)
    zero_row = jnp.zeros((1,) + jumps.shape[1:], jumps.dtype)
    padded_g = jnp.concatenate([zero_row, solved, zero_row], axis=0)
    my_sub = lax.axis_index("mer")
    g_lower = lax.dynamic_index_in_dim(padded_g, my_sub, 0, keepdims=False)
    g_upper = lax.dynamic_index_in_dim(padded_g, my_sub + 1, 0, keepdims=False)
    position = jnp.arange(points).astype(jnp.float32) / (points - 1)
    correction = (1.0 - position)[None, None, :, None] * g_lower[:, :, None, :] - position[
        None, None, :, None
    ] * g_upper[:, :, None, :]
    result = local + jnp.einsum("csip,rp->csir", correction, select, precision=highest)
    result = result * active[None, :, None, None]
    dof = float(modes * points * subdomains * width)
    part_re = jnp.einsum("kcsir,csir->k", basis_live, result, precision=highest)
    part_im = jnp.einsum(
        "ksir,sir->k", basis_live[:, 0], result[1], precision=highest
    ) - jnp.einsum("ksir,sir->k", basis_live[:, 1], result[0], precision=highest)
    summed_re, summed_im = lax.psum((part_re, part_im), ("mode", "mer"))
    proj_re = summed_re / dof
    proj_im = summed_im / dof
    rest_re = (
        result[0]
        - jnp.einsum("k,ksir->sir", proj_re, basis_live[:, 0], precision=highest)
        + jnp.einsum("k,ksir->sir", proj_im, basis_live[:, 1], precision=highest)
    )
    rest_im = (
        result[1]
        - jnp.einsum("k,ksir->sir", proj_re, basis_live[:, 1], precision=highest)
        - jnp.einsum("k,ksir->sir", proj_im, basis_live[:, 0], precision=highest)
    )
    rest_re, rest_im = (rest_re, rest_im)
    squares = lax.psum(jnp.sum(rest_re * rest_re) + jnp.sum(rest_im * rest_im), ("mode", "mer"))
    norm = jnp.sqrt(squares / dof + epsilon)
    new_vector = jnp.stack([rest_re, rest_im]) / norm
    return (new_vector, jnp.stack([proj_re, proj_im]), norm)


def solution(mesh):
    in_specs = (
        P(),
        P(),
        P(None, None, "mode", "mer", None),
        P(),
        P(None, "mer", None),
        P(None, "mer", None),
        P("mer", None),
        P(),
    )
    out_specs = (P(None, "mode", "mer", None), P(), P())
    return jax.shard_map(body, mesh=mesh, in_specs=in_specs, out_specs=out_specs, check_vma=False)
```

profile of v0, /device:TPU:0, one launch (start us, length us, event | category | flops | bytes accessed | tf_op | source)
XLA Modules:
  0.0 163.8 jit_solution(13731122193469821623)
XLA Ops:
  0.6 0.7 copy.13
  1.5 1.4 fusion.68
  3.6 2.0 %broadcast_multiply_fusion = f32[4,2,8,32,256]{4,3,2,1,0:T(8,128)S(1)} fusion(f32[4,2,8,32,256]{4,3,2,1,0:T(8,128)} %param.14, f32[8]{0:T(128)S(1)} %compare_convert_fusion.2), kind=kLoop, calls=%fused_computation.22 | loop fusion | flops 524288 | bytes 4194336 | tf_op jit(solution)/shard_map/mul | solution.py:57
  5.7 0.9 slice_bitcast_fusion.2
  6.5 5.7 %collective-permute-start.2 = (f32[2,8,32,256]{3,2,1,0:T(8,128)}, f32[2,8,32,256]{3,2,1,0:T(8,128)}, u32[]{:S(2)}, u32[]{:S(2)}) collective-permute-start(f32[2,8,32,256]{3,2,1,0:T(8,128)} %slice_bitcast_fusion.2), channel_id=1, source_target_pairs={{0,4},{4,8},{8,12},{12,16},{16,20},{20,24},{24,28},{1,5},{5,9},{9,... | collective-permute-start | bytes 1572872 | tf_op jit(solution)/shard_map/ppermute | solution.py:17
  12.2 1.3 collective-permute-start.3
  13.5 1.0 fusion.84
  14.5 1.5 collective-permute-start
  15.9 1.3 collective-permute-start.1
  17.3 1.4 fusion.33
  19.3 0.7 fusion.86
  20.5 1.2 slice_bitcast_fusion
  28.2 0.9 scatter-add.6
  29.0 1.6 scatter-add.9
  30.7 3.4 %collective-permute-done.2 = f32[2,8,32,256]{3,2,1,0:T(8,128)} collective-permute-done((f32[2,8,32,256]{3,2,1,0:T(8,128)}, f32[2,8,32,256]{3,2,1,0:T(8,128)}, u32[]{:S(2)}, u32[]{:S(2)}) %collective-permute-start.2) | collective-permute-done | bytes 524320 | tf_op jit(solution)/shard_map/ppermute | solution.py:17
  34.1 0.9 constant_dynamic-slice_fusion
  35.0 1.2 maximum_maximum_fusion
  36.2 0.9 slice_dynamic-update-slice_fusion
  37.2 0.8 fusion.7
  38.0 1.4 fusion.28
  41.0 5.4 %all-gather = f32[8,2,8,128]{3,2,1,0:T(8,128)S(1)} all-gather(f32[2,2,8,128]{3,2,1,0:T(8,128)S(1)} %pad_maximum_fusion), channel_id=2, replica_groups=mesh['mode'=8,'mer'=4] {'mer'}, dimensions={0}, use_global_device_ids=true | all-gather | bytes 81920 | tf_op jit(solution)/shard_map/all_gather | solution.py:87
  48.6 9.4 %fusion.9 = f32[4]{0:T(128)S(1)} fusion(f32[4,2,8,32,256]{4,3,2,1,0:T(8,128)S(1)} %broadcast_multiply_fusion, f32[2,8,32,256,1]{3,2,1,0,4:T(8,128)S(1)} %bitcast.208), kind=kOutput, calls=%fused_computation.16 | convolution fusion | flops 6291456 | bytes 2621456 | tf_op jit(solution)/shard_map/kcsir,csir->k/dot_general | solution.py:103
  58.0 4.8 %convolution_bitcast_fusion.4 = f32[4]{0:T(128)S(1)} fusion(f32[4,8,32,256]{3,2,1,0:T(8,128)S(1)} %copy-done, f32[8,32,256,1]{2,1,0,3:T(8,128)S(1)} %get-tuple-element.43), kind=kOutput, calls=%fused_computation.14 | convolution fusion | flops 3145728 | bytes 1310736 | tf_op jit(solution)/shard_map/ksir,sir->k/dot_general | solution.py:106
  62.8 5.0 %fusion.12 = f32[4]{0:T(128)S(1)} fusion(f32[4]{0:T(128)S(1)} %convolution_bitcast_fusion.4, f32[4,8,32,256]{3,2,1,0:T(8,128)S(1)} %get-tuple-element.39, f32[8,32,256,1]{2,1,0,3:T(8,128)S(1)} %get-tuple-element.42), kind=kOutput, calls=%fused_computation.17 | convolution fusion | flops 3145732 | bytes 1310752 | tf_op jit(solution)/shard_map/ksir,sir->k/dot_general | solution.py:104
  67.8 41.4 %all-reduce.1 = (f32[4]{0:T(128)S(1)}, f32[4]{0:T(128)S(1)}) all-reduce(f32[4]{0:T(128)S(1)} %fusion.12, f32[4]{0:T(128)S(1)} %fusion.9), channel_id=1, replica_groups=mesh['mode'=8,'mer'=4] {'mode','mer'}, use_global_device_ids=true, to_apply=%region_5.6 | all-reduce | flops 8 | bytes 64 | tf_op jit(solution)/shard_map/psum | solution.py:107
  109.2 2.3 %fusion.21 = f32[1,8,32,256]{3,0,2,1:T(1,128)S(1)} fusion(f32[4,8,32,256]{3,2,1,0:T(8,128)S(1)} %get-tuple-element.39, f32[4]{0:T(128)S(1)} %get-tuple-element.33), kind=kOutput, calls=%fused_computation.29 | convolution fusion | flops 3145732 | bytes 1310736 | tf_op jit(solution)/shard_map/k,ksir->sir/dot_general | solution.py:112
  111.5 2.3 %fusion.15 = f32[1,8,32,256]{3,0,2,1:T(1,128)S(1)} fusion(f32[4,8,32,256]{3,2,1,0:T(8,128)S(1)} %copy-done.1, f32[4]{0:T(128)S(1)} %get-tuple-element.33), kind=kOutput, calls=%fused_computation.23 | convolution fusion | flops 3145732 | bytes 1310736 | tf_op jit(solution)/shard_map/k,ksir->sir/dot_general | solution.py:117
  113.9 2.3 %fusion.17 = f32[1,8,32,256]{3,0,2,1:T(1,128)S(1)} fusion(f32[4,8,32,256]{3,2,1,0:T(8,128)S(1)} %copy-done.1, f32[4]{0:T(128)S(1)} %get-tuple-element.32), kind=kOutput, calls=%fused_computation.25 | convolution fusion | flops 3145732 | bytes 1310736 | tf_op jit(solution)/shard_map/k,ksir->sir/dot_general | solution.py:113
  116.2 2.3 %fusion.19 = f32[1,8,32,256]{3,0,2,1:T(1,128)S(1)} fusion(f32[4,8,32,256]{3,2,1,0:T(8,128)S(1)} %get-tuple-element.39, f32[4]{0:T(128)S(1)} %get-tuple-element.32), kind=kOutput, calls=%fused_computation.27 | convolution fusion | flops 3145732 | bytes 1310736 | tf_op jit(solution)/shard_map/k,ksir->sir/dot_general | solution.py:118
  118.6 0.8 multiply_reduce_fusion
  120.7 39.8 %psum.23 = f32[]{:T(128)} all-reduce(f32[]{:T(128)S(6)} %add.118), channel_id=1, replica_groups=mesh['mode'=8,'mer'=4] {'mode','mer'}, use_global_device_ids=true, to_apply=%region_8.9 | all-reduce | flops 1 | bytes 8 | tf_op jit(solution)/shard_map/psum | solution.py:121
  161.8 0.8 maximum_divide_fusion
  (59 shorter events, 7.1 us)
Async XLA Ops:
  3.6 13.7 %copy-start.6 = (f32[2,256,256]{2,1,0:T(8,128)S(1)}, f32[2,256,256]{2,1,0:T(8,128)}, u32[]{:S(2)}) copy-start(f32[2,256,256]{2,1,0:T(8,128)} %param.15) | copy-start | bytes 1572868
  5.6 13.0 %copy-start.8 = (f32[4,32,256]{2,1,0:T(8,128)S(1)}, f32[4,32,256]{2,1,0:T(8,128)}, u32[]{:S(2)}) copy-start(f32[4,32,256]{2,1,0:T(8,128)} %param.17) | copy-start | bytes 393220
  5.6 13.1 %copy-start.11 = (f32[2]{0:T(128)S(1)}, f32[2]{0:T(128)}, u32[]{:S(2)}) copy-start(f32[2]{0:T(128)} %param.19) | copy-start | bytes 28
  6.5 27.6 %collective-permute-start.2 = (f32[2,8,32,256]{3,2,1,0:T(8,128)}, f32[2,8,32,256]{3,2,1,0:T(8,128)}, u32[]{:S(2)}, u32[]{:S(2)}) collective-permute-start(f32[2,8,32,256]{3,2,1,0:T(8,128)} %slice_bitcast_fusion.2), channel_id=1, source_target_pairs={{0,4},{4,8},{8,12},{12,16},{16,20},{20,24},{24,28},{1,5},{5,9},{9,... | collective-permute-start | bytes 1572872 | tf_op jit(solution)/shard_map/ppermute | solution.py:17
  12.2 24.0 %collective-permute-start.3 = (f32[2,8,32,256]{3,2,1,0:T(8,128)}, f32[2,8,32,256]{3,2,1,0:T(8,128)}, u32[]{:S(2)}, u32[]{:S(2)}) collective-permute-start(f32[2,8,32,256]{3,2,1,0:T(8,128)} %slice_bitcast_fusion.2), channel_id=1, source_target_pairs={{4,0},{8,4},{12,8},{16,12},{20,16},{24,20},{28,24},{5,1},{9,5},{13... | collective-permute-start | bytes 1572872 | tf_op jit(solution)/shard_map/ppermute | solution.py:17
  14.5 13.7 %collective-permute-start = (f32[2,8,1,256]{3,2,1,0:T(1,128)S(1)}, f32[2,8,1,256]{3,2,1,0:T(1,128)S(1)}, u32[]{:S(2)}, u32[]{:S(2)}) collective-permute-start(f32[2,8,1,256]{3,2,1,0:T(1,128)S(1)} %get-tuple-element.47), channel_id=1, source_target_pairs={{0,1},{1,2},{2,3},{4,5},{5,6},{6,7},{8,9},{9,10},{10,11},{12,13},{... | collective-permute-start | bytes 49160 | tf_op jit(solution)/shard_map/ppermute | solution.py:27
  15.9 13.1 %collective-permute-start.1 = (f32[2,8,1,256]{3,2,1,0:T(1,128)S(1)}, f32[2,8,1,256]{3,2,1,0:T(1,128)S(1)}, u32[]{:S(2)}, u32[]{:S(2)}) collective-permute-start(f32[2,8,1,256]{3,2,1,0:T(1,128)S(1)} %get-tuple-element.46), channel_id=1, source_target_pairs={{1,0},{2,1},{3,2},{5,4},{6,5},{7,6},{9,8},{10,9},{11,10},{13,12},{... | collective-permute-start | bytes 49160 | tf_op jit(solution)/shard_map/ppermute | solution.py:28
  21.8 15.4 %copy-start.9 = (f32[2,32,32]{2,1,0:T(8,128)S(1)}, f32[2,32,32]{2,1,0:T(8,128)}, u32[]{:S(2)}) copy-start(f32[2,32,32]{2,1,0:T(8,128)} %param.16) | copy-start | bytes 24580
  30.7 6.5 %copy-start.4 = (f32[2,8,32,256]{3,2,1,0:T(8,128)S(1)}, f32[2,8,32,256]{3,2,1,0:T(8,128)}, u32[]{:S(2)}) copy-start(f32[2,8,32,256]{3,2,1,0:T(8,128)} %fusion.33) | copy-start | bytes 1572868
  30.7 6.5 %copy-start.5 = (f32[2,8,32,256]{3,2,1,0:T(8,128)S(1)}, f32[2,8,32,256]{3,2,1,0:T(8,128)}, u32[]{:S(2)}) copy-start(f32[2,8,32,256]{3,2,1,0:T(8,128)} %scatter-add.9) | copy-start | bytes 1572868
  35.0 2.9 %copy-start.10 = (f32[32,256]{1,0:T(8,128)S(1)}, f32[32,256]{1,0:T(8,128)}, u32[]{:S(2)}) copy-start(f32[32,256]{1,0:T(8,128)} %param.18) | copy-start | bytes 98308
  37.2 2.8 %copy-start.7 = (f32[2,256,256]{2,1,0:T(8,128)S(1)}, f32[2,256,256]{2,1,0:T(8,128)}, u32[]{:S(2)}) copy-start(f32[2,256,256]{2,1,0:T(8,128)} %param.15) | copy-start | bytes 1572868
  37.9 2.7 %copy-start.12 = (s32[128]{0:T(128)S(1)}, s32[128]{0:T(128)}, u32[]{:S(2)}) copy-start(s32[128]{0:T(128)} %param.13) | copy-start | bytes 1540
  48.6 9.5 %copy-start.2 = (f32[2,8,32,256]{3,2,1,0:T(8,128)}, f32[2,8,32,256]{3,2,1,0:T(8,128)S(1)}, u32[]{:S(2)}) copy-start(f32[2,8,32,256]{3,2,1,0:T(8,128)S(1)} %fusion.8) | copy-start | bytes 1572868
  48.6 9.4 %copy-start = (f32[4,8,32,256]{3,2,1,0:T(8,128)S(1)}, f32[4,8,32,256]{3,2,1,0:T(8,128)}, u32[]{:S(2)}) copy-start(f32[4,8,32,256]{3,2,1,0:T(8,128)} %get-tuple-element.38) | copy-start | bytes 3145732
  62.8 48.7 %copy-start.1 = (f32[4,8,32,256]{3,2,1,0:T(8,128)S(1)}, f32[4,8,32,256]{3,2,1,0:T(8,128)}, u32[]{:S(2)}) copy-start(f32[4,8,32,256]{3,2,1,0:T(8,128)} %get-tuple-element.38) | copy-start | bytes 3145732
  111.5 7.1 %copy-start.3 = (f32[2,8,32,256]{3,2,1,0:T(8,128)S(1)}, f32[2,8,32,256]{3,2,1,0:T(8,128)}, u32[]{:S(2)}) copy-start(f32[2,8,32,256]{3,2,1,0:T(8,128)} %copy-done.2) | copy-start | bytes 1572868
where the time goes:
time: 164 us
  blocking collectives  86.7 us (53%)
  matrix products  32.6 us (20%)
  other arithmetic  11.4 us (7%)
  local copies, waits for them, and re-layouts  10.2 us (6%)
  between operations  9.8 us (6%)
  starting transfers between devices  9.69 us (6%)
  waiting for transfers between devices  3.44 us (2%)
    psum x1, blocking collectives, body(): summed_re, summed_im = lax.psum((part_re, part_im), ('mode', 'mer'))  41.4 us
    psum x1, blocking collectives, body(): lax.psum(jnp.sum(rest_re * rest_re) + jnp.sum(rest_im * rest_im), ('mode'...  39.8 us
    dot_general x1, matrix products, body(): part_re = jnp.einsum('kcsir,csir->k', basis_live, result, precision=highest)  9.39 us
    ppermute x2, starting transfers between devices, passed_along(): return lax.ppermute(block, axis, route)  6.94 us
    all_gather x1, blocking collectives, body(): lax.all_gather(jnp.stack([top_trace, bottom_trace])[None], 'mer', axis=0,...  5.43 us
    dot_general x1, matrix products, body(): jnp.einsum('ksir,sir->k', basis_live[:, 0], result[1], precision=highest)  4.97 us
    dot_general x1, matrix products, body(): jnp.einsum('ksir,sir->k', basis_live[:, 1], result[0], precision=highest)  4.75 us
    ppermute x2, waiting for transfers between devices, passed_along(): return lax.ppermute(block, axis, route)  3.43 us
  transfers between devices with their start and end apart: 4, of which 1 were waited for; matrix products, arithmetic and copies ran while one was open for 7% of the time, Pallas kernels for 0%

commit v1 on v0

v1 whole, which is shorter than its diff:
```python
import functools

import jax
import jax.numpy as jnp
import numpy as np
from jax import lax
from jax.experimental import pallas as pl
from jax.experimental.pallas import tpu as pltpu
from jax.sharding import PartitionSpec as P

QUOTA = 840

penalty = 1.0
schur_diag = 2.2
epsilon = 1e-06

F32 = jnp.float32
BF16 = jnp.bfloat16


def split(x):
    hi = x.astype(BF16)
    return hi, (x - hi.astype(F32)).astype(BF16)


def mm(a, b):
    return lax.dot_general(a, b, (((1,), (0,)), ((), ())), preferred_element_type=F32)


def mmt(a, b):
    return lax.dot_general(a, b, (((1,), (1,)), ((), ())), preferred_element_type=F32)


def kernel(
    n_mode, n_mer, modes,
    cost, shift, iface, basis, radial, axial, flow, swirl,
    out, coef, norm,
    cur, ext, bas, rad, axl, flw, swl, ifc,
    stage, low, up, first, last, mlo, mhi,
    rh, rl, dh, dl, img, loc, trs, part, red_mer, red_mode,
    local_sem, halo_send, halo_recv, tr_send, tr_recv, ra_send, ra_recv, rb_send, rb_recv,
):
    krylov, _, slots, points, width = basis.shape
    rows = slots * points
    tiles = points // 8
    mode = lax.axis_index("mode")
    mer = lax.axis_index("mer")

    def at_mode(i):
        return {"mode": i}

    def at_mer(i):
        return {"mer": i}

    mesh_id = pl.DeviceIdType.MESH
    barrier = pltpu.get_barrier_semaphore()
    for i in range(1, n_mer):
        pl.semaphore_signal(barrier, inc=1, device_id=at_mer(lax.rem(mer + i, n_mer)), device_id_type=mesh_id)
    for i in range(1, n_mode):
        pl.semaphore_signal(barrier, inc=1, device_id=at_mode(lax.rem(mode + i, n_mode)), device_id_type=mesh_id)

    loads = [
        pltpu.make_async_copy(basis.at[krylov - 1], cur, local_sem.at[0]),
        pltpu.make_async_copy(axial, axl, local_sem.at[1]),
        pltpu.make_async_copy(iface, ifc, local_sem.at[2]),
        pltpu.make_async_copy(radial, rad, local_sem.at[3]),
        pltpu.make_async_copy(basis.at[krylov - 1], ext.at[:, 2 : 2 + slots], local_sem.at[4]),
        pltpu.make_async_copy(basis.at[0 : krylov - 1], bas, local_sem.at[5]),
        pltpu.make_async_copy(flow, flw, local_sem.at[6]),
        pltpu.make_async_copy(swirl, swl, local_sem.at[7]),
    ]
    for load in loads:
        load.start()

    least = mode * QUOTA

    def layout(k, carry):
        prefix, start, upto = carry
        start = start + (prefix < least).astype(jnp.int32)
        upto = upto + (prefix < least + QUOTA).astype(jnp.int32)
        return prefix + cost[k], start, upto

    zero = jnp.int32(0)
    _, start, upto = lax.fori_loop(0, modes, layout, (zero, zero, zero), unroll=8)
    count = upto - start
    ending = jnp.clip(count, 2, slots) - 2

    loads[0].wait()
    for c in range(2):
        for i in range(2):
            stage[c, i] = cur[c, ending + i]
        for s in range(slots):
            first[c, s : s + 1, :] = cur[c, s, 0:1, :]
            last[c, s : s + 1, :] = cur[c, s, points - 1 : points, :]

    def halo(which, src, dst, device):
        return pltpu.make_async_remote_copy(
            src_ref=src, dst_ref=dst, send_sem=halo_send.at[which], recv_sem=halo_recv.at[which],
            device_id=device, device_id_type=mesh_id,
        )

    to_next = halo(0, stage, low, at_mode(lax.rem(mode + 1, n_mode)))
    to_prev = halo(1, cur.at[:, 0:2], up, at_mode(lax.rem(mode + n_mode - 1, n_mode)))
    to_right = halo(2, last, mlo, at_mer(lax.rem(mer + 1, n_mer)))
    to_left = halo(3, first, mhi, at_mer(lax.rem(mer + n_mer - 1, n_mer)))
    has_next, has_prev = mode < n_mode - 1, mode > 0
    has_right, has_left = mer < n_mer - 1, mer > 0
    pl.semaphore_wait(barrier, n_mer - 1 + n_mode - 1)
    for there, copy in ((has_next, to_next), (has_prev, to_prev), (has_right, to_right), (has_left, to_left)):

        @pl.when(there)
        def _(copy=copy):
            copy.start()

    loads[1].wait()
    col = lax.broadcasted_iota(jnp.int32, (points, width), 1)
    row = lax.broadcasted_iota(jnp.int32, (points, width), 0)
    spread = col == row
    for s in range(1, slots):
        spread = jnp.logical_or(spread, col == row + s * points)
    spread = jnp.where(spread, 1.0, 0.0).astype(BF16)
    col8 = lax.broadcasted_iota(jnp.int32, (slots, width), 1)
    base8 = lax.broadcasted_iota(jnp.int32, (slots, width), 0) * points
    mine8 = jnp.logical_and(col8 >= base8, col8 < base8 + points)
    for k in range(2):
        for part_of, to in zip(split(axl[k]), (dh, dl)):
            wide = mm(part_of, spread)
            for s in range(slots):
                block = jnp.logical_and(col >= s * points, col < (s + 1) * points)
                to[k, s * points : (s + 1) * points, :] = jnp.where(block, wide, 0.0).astype(BF16)
            if k == 1:
                top = jnp.where(mine8, jnp.broadcast_to(wide[points - 1 : points], (slots, width)), 0.0)
                bottom = jnp.where(mine8, jnp.broadcast_to(wide[0:1], (slots, width)), 0.0)
                to[k, rows : rows + 2 * slots, :] = jnp.concatenate([top, bottom], axis=0).astype(BF16)

    loads[2].wait()
    places = lax.broadcasted_iota(jnp.int32, (width, ifc.shape[1]), 0)
    chosen = jnp.where(places == ifc[...], 1.0, 0.0).astype(BF16)
    mask = mmt(jnp.ones((8, ifc.shape[1]), BF16), chosen)

    loads[3].wait()
    for k in range(2):
        rh[k], rl[k] = split(rad[k])
    for c in range(2):
        xh, xl = split(cur[c].reshape(rows, width))
        total = mmt(xh, rh[0]) + mmt(xl, rh[0]) + mmt(xh, rl[0])
        total = total + mm(dh[0, 0:rows], xh) + mm(dl[0, 0:rows], xh) + mm(dh[0, 0:rows], xl)
        img[c] = total.reshape(slots, points, width)

    loads[5].wait()
    pairs = [(i, j) for i in range(krylov) for j in range(i, krylov)]
    cross = [(i, j) for i in range(krylov) for j in range(i + 1, krylov)]

    def fold(x):
        half = x[:, 0:128]
        for at in range(128, width, 128):
            half = half + x[:, at : at + 128]
        return jnp.sum(half, axis=0, keepdims=True)

    def gram(s, carry):
        carry = list(carry)
        live = s < count
        for t in range(tiles):
            z = pl.ds(t * 8, 8)
            q = [[bas[j, c, s, z, :] for c in range(2)] for j in range(krylov - 1)]
            q.append([cur[c, s, z, :] for c in range(2)])
            q = [[jnp.where(live, x, 0.0) for x in both] for both in q]
            for n, (i, j) in enumerate(pairs):
                carry[n] = carry[n] + (q[i][0] * q[j][0] + q[i][1] * q[j][1])
            for n, (i, j) in enumerate(cross):
                n += len(pairs)
                carry[n] = carry[n] + (q[i][0] * q[j][1] - q[i][1] * q[j][0])
        return tuple(carry)

    empty = jnp.zeros((8, width), F32)
    grams = lax.fori_loop(0, slots, gram, (empty,) * (len(pairs) + len(cross)))
    n_inner = 2 * krylov + 1
    part[...] = jnp.zeros(part.shape, F32)
    for n, x in enumerate(grams):
        part[n_inner + n : n_inner + n + 1, :] = fold(x)

    loads[4].wait()
    loads[6].wait()
    loads[7].wait()

    @pl.when(has_prev)
    def _():
        to_next.wait_recv()
        ext[:, 0:2] = low[...]

    @pl.when(jnp.logical_not(has_prev))
    def _():
        ext[:, 0:2] = jnp.zeros(low.shape, F32)

    @pl.when(has_next)
    def _():
        to_prev.wait_recv()
        for i in range(2):
            ext[:, 2 + slots + i] = jnp.where(upto + i < modes, up[:, i], 0.0)

    @pl.when(jnp.logical_not(has_next))
    def _():
        ext[:, 2 + slots : 4 + slots] = jnp.zeros(up.shape, F32)

    @pl.when(has_left)
    def _():
        to_right.wait_recv()

    @pl.when(jnp.logical_not(has_left))
    def _():
        mlo[...] = jnp.zeros(mlo.shape, F32)

    @pl.when(has_right)
    def _():
        to_left.wait_recv()

    @pl.when(jnp.logical_not(has_right))
    def _():
        mhi[...] = jnp.zeros(mhi.shape, F32)

    sig_re, sig_im = shift[0], shift[1]
    sub8 = lax.broadcasted_iota(jnp.int32, (8, width), 0)
    for s in range(slots):
        wave = (start + s).astype(F32) / modes
        at = []
        for d in (-2, -1, 1, 2):
            over = s + d - count
            at.append(jnp.where(over < 0, 2 + s + d, 2 + slots + jnp.minimum(over, 1)))
        for t in range(tiles):
            z = slice(t * 8, (t + 1) * 8)
            spin = sig_im - wave * swl[z, :]
            x = (cur[0, s, z, :], cur[1, s, z, :])
            coupling = [flw[i, z, :] for i in range(4)]
            for c in range(2):
                acc = img[c, s, z, :]
                for i in range(4):
                    acc = acc + coupling[i] * ext[c, at[i], z, :]
                turn = spin * x[1] if c == 0 else -(spin * x[0])
                acc = acc - sig_re * x[c] + turn
                if t == 0:
                    acc = acc + jnp.where(sub8 == 0, penalty * mlo[c, s : s + 1, :], 0.0)
                if t == tiles - 1:
                    acc = acc + jnp.where(sub8 == 7, penalty * mhi[c, s : s + 1, :], 0.0)
                img[c, s, z, :] = acc

    inner = []
    for c in range(2):
        xh, xl = split(img[c].reshape(rows, width))
        y = mm(dh[1], xh) + mm(dl[1], xh) + mm(dh[1], xl)
        ends = split(y[rows : rows + 2 * slots])
        both = mmt(ends[0], rh[1]) + mmt(ends[1], rh[1]) + mmt(ends[0], rl[1])
        trs[mer, 0, c] = both[0:slots]
        trs[mer, 1, c] = both[slots : 2 * slots]
        inner.append(y[0:rows])

    def trace(i, slot, to):
        return pltpu.make_async_remote_copy(
            src_ref=trs.at[slot], dst_ref=trs.at[slot], send_sem=tr_send.at[i], recv_sem=tr_recv.at[i],
            device_id=at_mer(to), device_id_type=mesh_id,
        )

    for i in range(1, n_mer):
        trace(i, mer, lax.rem(mer + i, n_mer)).start()
    for c in range(2):
        yh, yl = split(inner[c])
        loc[c] = (mmt(yh, rh[1]) + mmt(yl, rh[1]) + mmt(yh, rl[1])).reshape(slots, points, width)
    for i in range(1, n_mer):
        trace(i, lax.rem(mer + n_mer - i, n_mer), mer).wait_recv()

    count_j = n_mer - 1
    inverse = np.linalg.inv(schur_diag * np.eye(count_j) - np.eye(count_j, k=1) - np.eye(count_j, k=-1))
    inverse = np.pad(inverse, ((1, 1), (0, 0)))
    jumps = [[trs[j, 0, c] - trs[j + 1, 1, c] for c in range(2)] for j in range(count_j)]

    def weight(side, j):
        value = jnp.float32(0.0)
        for b in range(n_mer):
            value = jnp.where(mer == b, jnp.float32(inverse[b + side, j]), value)
        return value

    sides = []
    for side in range(2):
        weights = [weight(side, j) for j in range(count_j)]
        sides.append([mask * sum(w * jump[c] for w, jump in zip(weights, jumps)) for c in range(2)])

    accs = [empty] * n_inner
    height = lax.broadcasted_iota(jnp.int32, (8, width), 0)
    for s in range(slots):
        live = s < count
        for t in range(tiles):
            z = slice(t * 8, (t + 1) * 8)
            position = (height + t * 8).astype(F32) / (points - 1)
            w = []
            for c in range(2):
                x = loc[c, s, z, :] + (1.0 - position) * sides[0][c][s : s + 1] - position * sides[1][c][s : s + 1]
                x = jnp.where(live, x, 0.0)
                loc[c, s, z, :] = x
                w.append(x)
            for j in range(krylov):
                src = cur if j == krylov - 1 else bas.at[j]
                re, im = src[0, s, z, :], src[1, s, z, :]
                accs[j] = accs[j] + (re * w[0] + im * w[1])
                accs[krylov + j] = accs[krylov + j] + (re * w[1] - im * w[0])
            accs[2 * krylov] = accs[2 * krylov] + (w[0] * w[0] + w[1] * w[1])
    for n, x in enumerate(accs):
        part[n : n + 1, :] = fold(x)

    def share(buffer, sends, recvs, i, slot, device):
        return pltpu.make_async_remote_copy(
            src_ref=buffer.at[slot], dst_ref=buffer.at[slot], send_sem=sends.at[i], recv_sem=recvs.at[i],
            device_id=device, device_id_type=mesh_id,
        )

    red_mer[mer] = part[...]
    for i in range(1, n_mer):
        share(red_mer, ra_send, ra_recv, i, mer, at_mer(lax.rem(mer + i, n_mer))).start()
    for i in range(1, n_mer):
        share(red_mer, ra_send, ra_recv, i, lax.rem(mer + n_mer - i, n_mer), at_mer(mer)).wait_recv()
    total = red_mer[0]
    for i in range(1, n_mer):
        total = total + red_mer[i]
    red_mode[mode] = total
    for i in range(1, n_mode):
        share(red_mode, rb_send, rb_recv, i, mode, at_mode(lax.rem(mode + i, n_mode))).start()
    for i in range(1, n_mode):
        share(red_mode, rb_send, rb_recv, i, lax.rem(mode + n_mode - i, n_mode), at_mode(mode)).wait_recv()
    total = red_mode[0]
    for i in range(1, n_mode):
        total = total + red_mode[i]
    dof = float(modes * points * n_mer * width)
    total = jnp.sum(total, axis=1, keepdims=True) / dof
    one = [total[n : n + 1, :] for n in range(n_inner + len(pairs) + len(cross))]
    c_re, c_im = one[0:krylov], one[krylov : 2 * krylov]
    square = one[2 * krylov]
    for j in range(krylov):
        square = square - 2.0 * (c_re[j] * c_re[j] + c_im[j] * c_im[j])
    for n, (i, j) in enumerate(pairs):
        both = c_re[i] * c_re[j] + c_im[i] * c_im[j]
        square = square + (1.0 if i == j else 2.0) * both * one[n_inner + n]
    for n, (i, j) in enumerate(cross):
        both = c_re[i] * c_im[j] - c_im[i] * c_re[j]
        square = square - 2.0 * both * one[n_inner + len(pairs) + n]
    size = jnp.sqrt(jnp.maximum(square, 0.0) + epsilon)
    norm[...] = size
    lane = lax.broadcasted_iota(jnp.int32, coef.shape, 1)
    side = lax.broadcasted_iota(jnp.int32, coef.shape, 0)
    table = jnp.zeros(coef.shape, F32)
    for j in range(krylov):
        table = jnp.where(lane == j, jnp.where(side == 0, c_re[j], c_im[j]), table)
    coef[...] = table

    scale = 1.0 / size
    scaled_re = [jnp.broadcast_to(x * scale, (8, width)) for x in c_re]
    scaled_im = [jnp.broadcast_to(x * scale, (8, width)) for x in c_im]
    scale = jnp.broadcast_to(scale, (8, width))
    for s in range(slots):
        live = s < count
        for t in range(tiles):
            z = slice(t * 8, (t + 1) * 8)
            new_re = loc[0, s, z, :] * scale
            new_im = loc[1, s, z, :] * scale
            for j in range(krylov):
                src = cur if j == krylov - 1 else bas.at[j]
                re, im = src[0, s, z, :], src[1, s, z, :]
                new_re = new_re - (scaled_re[j] * re - scaled_im[j] * im)
                new_im = new_im - (scaled_re[j] * im + scaled_im[j] * re)
            out[0, s, z, :] = jnp.where(live, new_re, 0.0)
            out[1, s, z, :] = jnp.where(live, new_im, 0.0)

    for there, copy in ((has_next, to_next), (has_prev, to_prev), (has_right, to_right), (has_left, to_left)):

        @pl.when(there)
        def _(copy=copy):
            copy.wait_send()

    for i in range(1, n_mer):
        trace(i, mer, lax.rem(mer + i, n_mer)).wait_send()
        share(red_mer, ra_send, ra_recv, i, mer, at_mer(lax.rem(mer + i, n_mer))).wait_send()
    for i in range(1, n_mode):
        share(red_mode, rb_send, rb_recv, i, mode, at_mode(lax.rem(mode + i, n_mode))).wait_send()


def body(n_mode, n_mer, mode_cost, iface_index, basis, radial, axial, flow_coupling, swirl, shift):
    krylov, _, slots, points, width = basis.shape
    modes = mode_cost.shape[0]
    rows = slots * points
    sums = 2 * krylov + 1 + krylov * krylov
    sums = (sums + 7) // 8 * 8
    field = (2, slots, points, width)
    pair = (2, 2, points, width)
    ends = (2, slots, width)
    smem = pl.BlockSpec(memory_space=pltpu.SMEM)
    hbm = pl.BlockSpec(memory_space=pl.ANY)
    vmem = pl.BlockSpec(memory_space=pltpu.VMEM)
    dma = pltpu.SemaphoreType.DMA
    new_vector, coeffs, norm = pl.pallas_call(
        functools.partial(kernel, n_mode, n_mer, modes),
        out_shape=[
            jax.ShapeDtypeStruct(field, F32),
            jax.ShapeDtypeStruct((2, krylov), F32),
            jax.ShapeDtypeStruct((1, 1), F32),
        ],
        in_specs=[smem, smem] + [hbm] * 6,
        out_specs=[vmem] * 3,
        scratch_shapes=[
            pltpu.VMEM(field, F32),
            pltpu.VMEM((2, slots + 4, points, width), F32),
            pltpu.VMEM((krylov - 1,) + field, F32),
            pltpu.VMEM(radial.shape, F32),
            pltpu.VMEM(axial.shape, F32),
            pltpu.VMEM(flow_coupling.shape, F32),
            pltpu.VMEM(swirl.shape, F32),
            pltpu.VMEM((1, iface_index.shape[0]), jnp.int32),
            pltpu.VMEM(pair, F32),
            pltpu.VMEM(pair, F32),
            pltpu.VMEM(pair, F32),
            pltpu.VMEM(ends, F32),
            pltpu.VMEM(ends, F32),
            pltpu.VMEM(ends, F32),
            pltpu.VMEM(ends, F32),
            pltpu.VMEM(radial.shape, BF16),
            pltpu.VMEM(radial.shape, BF16),
            pltpu.VMEM((2, rows + 2 * slots, rows), BF16),
            pltpu.VMEM((2, rows + 2 * slots, rows), BF16),
            pltpu.VMEM(field, F32),
            pltpu.VMEM(field, F32),
            pltpu.VMEM((n_mer, 2) + ends, F32),
            pltpu.VMEM((sums, 128), F32),
            pltpu.VMEM((n_mer, sums, 128), F32),
            pltpu.VMEM((n_mode, sums, 128), F32),
            dma((8,)),
            dma((4,)),
            dma((4,)),
            dma((n_mer,)),
            dma((n_mer,)),
            dma((n_mer,)),
            dma((n_mer,)),
            dma((n_mode,)),
            dma((n_mode,)),
        ],
        compiler_params=pltpu.CompilerParams(
            collective_id=0, has_side_effects=True, vmem_limit_bytes=60 * 1024 * 1024
        ),
    )(mode_cost, shift, iface_index[None, :], basis, radial, axial, flow_coupling, swirl)
    return new_vector, coeffs, norm.reshape(())


def solution(mesh):
    in_specs = (
        P(),
        P(),
        P(None, None, "mode", "mer", None),
        P(),
        P(None, "mer", None),
        P(None, "mer", None),
        P("mer", None),
        P(),
    )
    out_specs = (P(None, "mode", "mer", None), P(), P())
    program = functools.partial(body, mesh.shape["mode"], mesh.shape["mer"])
    return jax.shard_map(program, mesh=mesh, in_specs=in_specs, out_specs=out_specs, check_vma=False)
```

time: 164 us -> 32.1 us (0.20)
  blocking collectives: 86.7 us -> 0 us
  matrix products: 32.6 us -> 0 us
  Pallas kernels: 0 us -> 26.4 us
  other arithmetic: 11.4 us -> 0 us
  starting transfers between devices: 9.69 us -> 0 us
  between operations: 9.8 us -> 2.41 us
  local copies, waits for them, and re-layouts: 10.2 us -> 3.08 us
  waiting for transfers between devices: 3.44 us -> 0 us
    psum x2 -> x0, blocking collectives: 81.3 us -> none  [the longest x1 41.4 us: body(): summed_re, summed_im = lax.psum((part_re, part_im), ('mode', 'mer'))]
    dot_general x14 -> x0, matrix products: 32.6 us -> none  [the longest x1 9.39 us: body(): part_re = jnp.einsum('kcsir,csir->k', basis_live, result, precision=highest)]
    pallas_call x0 -> x1, Pallas kernels: none -> 26.4 us  [body(): pl.pallas_call(functools.partial(kernel, n_mode, n_mer, modes), out_shape...]
    ppermute x4 -> x0, starting transfers between devices: 9.69 us -> none  [the longest x2 6.94 us: passed_along(): return lax.ppermute(block, axis, route)]
    all_gather x1 -> x0, blocking collectives: 5.43 us -> none  [body(): lax.all_gather(jnp.stack([top_trace, bottom_trace])[None], 'mer', axis=0,...]
    ppermute x4 -> x0, waiting for transfers between devices: 3.44 us -> none  [the longest x2 3.43 us: passed_along(): return lax.ppermute(block, axis, route)]
    unnamed x27 -> x2, local copies, waits for them, and re-layouts: 0.07 us -> 3.08 us
    slice x5 -> x0, local copies, waits for them, and re-layouts: 2.86 us -> none  [the longest x2 1.25 us: solve_interface(): return lax.linalg.tridiagonal_solve(below, diagonal, above, rhs)]
  transfers between devices with their start and end apart: 4 -> 0, of which waited for: 1 -> 0; matrix products, arithmetic and copies ran while one was open for 7% -> 0% of each run, Pallas kernels for 0% -> 0%
where the time goes in v1:
time: 32.1 us; the launch traced here: 31.9 us
  Pallas kernels  26.4 us (82%)
  local copies, waits for them, and re-layouts  3.08 us (10%)
  between operations  2.41 us (8%)
    pallas_call x1, Pallas kernels, body(): pl.pallas_call(functools.partial(kernel, n_mode, n_mer, modes), out_shape...  26.4 us
    unnamed x2, local copies, waits for them, and re-layouts  3.08 us

profile of v1, /device:TPU:0, one launch (start us, length us, event | category | flops | bytes accessed | tf_op | source)
XLA Modules:
  0.0 31.9 jit_solution(14367307034582475731)
XLA Ops:
  0.6 26.4 %shard_map.103 = (f32[2,8,32,256]{3,2,1,0:T(8,128)}, f32[2,4]{1,0:T(2,128)}, f32[1,1]{1,0:T(1,128)}) custom-call(s32[32]{0:T(128)} %cost.1, f32[2]{0:T(128)} %shift.1, s32[1,128]{1,0:T(1,128)} %bitcast.2, f32[4,2,8,32,256]{4,3,2,1,0:T(8,128)} %basis.1, f32[2,256,256]{2,1,0:T(8,128)} %radial.1, f32[2,32,32]{2,1,0:T(8,128)} %axial.1, f32[4,32,256]{2,1,0:T(8,128)} %flow.1, ...), custom_call_target="tpu_custom_call" | custom-call | tf_op jit(solution)/shard_map/pallas_call | solution.py:396
  27.0 1.9 %copy.14 = f32[2,8,32,256]{3,2,1,0:T(8,128)} copy(f32[2,8,32,256]{3,2,1,0:T(8,128)} %get-tuple-element.12) | data formatting | bytes 1048576
  28.9 1.2 %copy.15 = f32[2,4]{1,0:T(2,128)} copy(f32[2,4]{1,0:T(2,128)} %get-tuple-element.13) | data formatting | bytes 64

commit v2 on v1

--- a/solution.py
+++ b/solution.py
@@ -31,14 +31,91 @@
     return lax.dot_general(a, b, (((1,), (1,)), ((), ())), preferred_element_type=F32)
 
 
+def diagonal(size):
+    row = lax.broadcasted_iota(jnp.int32, (size, 128), 0)
+    return row == lax.broadcasted_iota(jnp.int32, (size, 128), 1)
+
+
+def to_row(column):
+    return jnp.sum(jnp.where(diagonal(column.shape[0]), column, 0.0), axis=0, keepdims=True)
+
+
+def to_column(row, size):
+    return jnp.sum(jnp.where(diagonal(size), row, 0.0), axis=1, keepdims=True)
+
+
+def finish(dof, basis, w_in, stats, out, coef, norm, bas, w, fresh, in_sem, w_sem, out_sem):
+    krylov, _, slots, points, width = basis.shape
+    tiles = points // 8
+    pairs = [(i, j) for i in range(krylov) for j in range(i, krylov)]
+    cross = [(i, j) for i in range(krylov) for j in range(i + 1, krylov)]
+    n_inner = 2 * krylov + 1
+    sums = n_inner + len(pairs) + len(cross)
+    half = slots // 2
+    ins, outs = [], []
+    for n in range(2):
+        at = pl.ds(n * half, half)
+        ins.append(pltpu.make_async_copy(basis.at[:, :, at], bas.at[:, :, at], in_sem.at[n]))
+        ins.append(pltpu.make_async_copy(w_in.at[:, at], w.at[:, at], w_sem.at[n]))
+        outs.append(pltpu.make_async_copy(fresh.at[:, at], out.at[:, at], out_sem.at[n]))
+    for copy in ins:
+        copy.start()
+    count = stats[:, 127:128]
+    total = to_column(stats[...], (sums + 7) // 8 * 8) / dof
+    one = [total[n : n + 1, :] for n in range(sums)]
+    c_re, c_im = one[0:krylov], one[krylov : 2 * krylov]
+    square = one[2 * krylov]
+    for j in range(krylov):
+        square = square - 2.0 * (c_re[j] * c_re[j] + c_im[j] * c_im[j])
+    for n, (i, j) in enumerate(pairs):
+        both = c_re[i] * c_re[j] + c_im[i] * c_im[j]
+        square = square + (1.0 if i == j else 2.0) * both * one[n_inner + n]
+    for n, (i, j) in enumerate(cross):
+        both = c_re[i] * c_im[j] - c_im[i] * c_re[j]
+        square = square - 2.0 * both * one[n_inner + len(pairs) + n]
+    size = jnp.sqrt(jnp.maximum(square, 0.0) + epsilon)
+    norm[...] = size
+    lane = lax.broadcasted_iota(jnp.int32, coef.shape, 1)
+    side = lax.broadcasted_iota(jnp.int32, coef.shape, 0)
+    table = jnp.zeros(coef.shape, F32)
+    for j in range(krylov):
+        table = jnp.where(lane == j, jnp.where(side == 0, c_re[j], c_im[j]), table)
+    coef[...] = table
+
+    scale = 1.0 / size
+    scaled_re = [jnp.broadcast_to(x * scale, (8, width)) for x in c_re]
+    scaled_im = [jnp.broadcast_to(x * scale, (8, width)) for x in c_im]
+    scale = jnp.broadcast_to(scale, (8, width))
+    live_to = jnp.broadcast_to(count, (8, width))
+    for s in range(slots):
+        if s % half == 0:
+            ins[s // half * 2].wait()
+            ins[s // half * 2 + 1].wait()
+        live = live_to > s
+        for t in range(tiles):
+            z = slice(t * 8, (t + 1) * 8)
+            new_re = w[0, s, z, :] * scale
+            new_im = w[1, s, z, :] * scale
+            for j in range(krylov):
+                re, im = bas[j, 0, s, z, :], bas[j, 1, s, z, :]
+                new_re = new_re - (scaled_re[j] * re - scaled_im[j] * im)
+                new_im = new_im - (scaled_re[j] * im + scaled_im[j] * re)
+            fresh[0, s, z, :] = jnp.where(live, new_re, 0.0)
+            fresh[1, s, z, :] = jnp.where(live, new_im, 0.0)
+        if s % half == half - 1:
+            outs[s // half].start()
+    for copy in outs:
+        copy.wait()
+
+
 def kernel(
     n_mode, n_mer, modes,
     cost, shift, iface, basis, radial, axial, flow, swirl,
-    out, coef, norm,
-    cur, ext, bas, rad, axl, flw, swl, ifc,
+    w_out, stats,
+    cur, bas, rad, axl, flw, swl, ifc,
     stage, low, up, first, last, mlo, mhi,
     rh, rl, dh, dl, img, loc, trs, part, red_mer, red_mode,
-    local_sem, halo_send, halo_recv, tr_send, tr_recv, ra_send, ra_recv, rb_send, rb_recv,
+    local_sem, w_sem, halo_send, halo_recv, tr_send, tr_recv, ra_send, ra_recv, rb_send, rb_recv,
 ):
     krylov, _, slots, points, width = basis.shape
     rows = slots * points
@@ -64,10 +141,9 @@
         pltpu.make_async_copy(axial, axl, local_sem.at[1]),
         pltpu.make_async_copy(iface, ifc, local_sem.at[2]),
         pltpu.make_async_copy(radial, rad, local_sem.at[3]),
-        pltpu.make_async_copy(basis.at[krylov - 1], ext.at[:, 2 : 2 + slots], local_sem.at[4]),
-        pltpu.make_async_copy(basis.at[0 : krylov - 1], bas, local_sem.at[5]),
-        pltpu.make_async_copy(flow, flw, local_sem.at[6]),
-        pltpu.make_async_copy(swirl, swl, local_sem.at[7]),
+        pltpu.make_async_copy(flow, flw, local_sem.at[4]),
+        pltpu.make_async_copy(swirl, swl, local_sem.at[5]),
+        pltpu.make_async_copy(basis.at[0 : krylov - 1], bas, local_sem.at[6]),
     ]
     for load in loads:
         load.start()
@@ -147,7 +223,51 @@
         total = total + mm(dh[0, 0:rows], xh) + mm(dl[0, 0:rows], xh) + mm(dh[0, 0:rows], xl)
         img[c] = total.reshape(slots, points, width)
 
+    loads[4].wait()
     loads[5].wait()
+
+    @pl.when(has_left)
+    def _():
+        to_right.wait_recv()
+
+    @pl.when(jnp.logical_not(has_left))
+    def _():
+        mlo[...] = jnp.zeros(mlo.shape, F32)
+
+    @pl.when(has_right)
+    def _():
+        to_left.wait_recv()
+
+    @pl.when(jnp.logical_not(has_right))
+    def _():
+        mhi[...] = jnp.zeros(mhi.shape, F32)
+
+    sig_re, sig_im = shift[0], shift[1]
+    sub8 = lax.broadcasted_iota(jnp.int32, (8, width), 0)
+    offsets = (-2, -1, 1, 2)
+    for s in range(slots):
+        wave = (start + s).astype(F32) / modes
+        for t in range(tiles):
+            z = slice(t * 8, (t + 1) * 8)
+            spin = sig_im - wave * swl[z, :]
+            x = (cur[0, s, z, :], cur[1, s, z, :])
+            for c in range(2):
+                acc = img[c, s, z, :]
+                for i, d in enumerate(offsets):
+                    if 0 <= s + d < slots:
+                        other = cur[c, s + d, z, :]
+                        if d > 0:
+                            other = jnp.where(s + d < count, other, 0.0)
+                        acc = acc + flw[i, z, :] * other
+                turn = spin * x[1] if c == 0 else -(spin * x[0])
+                acc = acc - sig_re * x[c] + turn
+                if t == 0:
+                    acc = acc + jnp.where(sub8 == 0, penalty * mlo[c, s : s + 1, :], 0.0)
+                if t == tiles - 1:
+                    acc = acc + jnp.where(sub8 == 7, penalty * mhi[c, s : s + 1, :], 0.0)
+                img[c, s, z, :] = acc
+
+    loads[6].wait()
     pairs = [(i, j) for i in range(krylov) for j in range(i, krylov)]
     cross = [(i, j) for i in range(krylov) for j in range(i + 1, krylov)]
 
@@ -179,69 +299,24 @@
     for n, x in enumerate(grams):
         part[n_inner + n : n_inner + n + 1, :] = fold(x)
 
-    loads[4].wait()
-    loads[6].wait()
-    loads[7].wait()
-
     @pl.when(has_prev)
     def _():
         to_next.wait_recv()
-        ext[:, 0:2] = low[...]
-
-    @pl.when(jnp.logical_not(has_prev))
-    def _():
-        ext[:, 0:2] = jnp.zeros(low.shape, F32)
+        for c in range(2):
+            img[c, 0] = img[c, 0] + (flw[0] * low[c, 0] + flw[1] * low[c, 1])
+            img[c, 1] = img[c, 1] + flw[0] * low[c, 1]
 
     @pl.when(has_next)
     def _():
         to_prev.wait_recv()
-        for i in range(2):
-            ext[:, 2 + slots + i] = jnp.where(upto + i < modes, up[:, i], 0.0)
-
-    @pl.when(jnp.logical_not(has_next))
-    def _():
-        ext[:, 2 + slots : 4 + slots] = jnp.zeros(up.shape, F32)
-
-    @pl.when(has_left)
-    def _():
-        to_right.wait_recv()
-
-    @pl.when(jnp.logical_not(has_left))
-    def _():
-        mlo[...] = jnp.zeros(mlo.shape, F32)
-
-    @pl.when(has_right)
-    def _():
-        to_left.wait_recv()
-
-    @pl.when(jnp.logical_not(has_right))
-    def _():
-        mhi[...] = jnp.zeros(mhi.shape, F32)
-
-    sig_re, sig_im = shift[0], shift[1]
-    sub8 = lax.broadcasted_iota(jnp.int32, (8, width), 0)
-    for s in range(slots):
-        wave = (start + s).astype(F32) / modes
-        at = []
-        for d in (-2, -1, 1, 2):
-            over = s + d - count
-            at.append(jnp.where(over < 0, 2 + s + d, 2 + slots + jnp.minimum(over, 1)))
-        for t in range(tiles):
-            z = slice(t * 8, (t + 1) * 8)
-            spin = sig_im - wave * swl[z, :]
-            x = (cur[0, s, z, :], cur[1, s, z, :])
-            coupling = [flw[i, z, :] for i in range(4)]
-            for c in range(2):
-                acc = img[c, s, z, :]
-                for i in range(4):
-                    acc = acc + coupling[i] * ext[c, at[i], z, :]
-                turn = spin * x[1] if c == 0 else -(spin * x[0])
-                acc = acc - sig_re * x[c] + turn
-                if t == 0:
-                    acc = acc + jnp.where(sub8 == 0, penalty * mlo[c, s : s + 1, :], 0.0)
-                if t == tiles - 1:
-                    acc = acc + jnp.where(sub8 == 7, penalty * mhi[c, s : s + 1, :], 0.0)
-                img[c, s, z, :] = acc
+        for c in range(2):
+            one_up = jnp.where(upto < modes, up[c, 0], 0.0)
+            two_up = jnp.where(upto + 1 < modes, up[c, 1], 0.0)
+            on_last = flw[2] * one_up + flw[3] * two_up
+            on_second = flw[3] * one_up
+            for s in range(slots):
+                term = jnp.where(s == count - 1, on_last, jnp.where(s == count - 2, on_second, 0.0))
+                img[c, s] = img[c, s] + term
 
     inner = []
     for c in range(2):
@@ -302,6 +377,7 @@
                 accs[j] = accs[j] + (re * w[0] + im * w[1])
                 accs[krylov + j] = accs[krylov + j] + (re * w[1] - im * w[0])
             accs[2 * krylov] = accs[2 * krylov] + (w[0] * w[0] + w[1] * w[1])
+        pltpu.make_async_copy(loc.at[:, s], w_out.at[:, s], w_sem.at[s]).start()
     for n, x in enumerate(accs):
         part[n : n + 1, :] = fold(x)
 
@@ -311,7 +387,7 @@
             device_id=device, device_id_type=mesh_id,
         )
 
-    red_mer[mer] = part[...]
+    red_mer[mer] = to_row(jnp.sum(part[...], axis=1, keepdims=True))
     for i in range(1, n_mer):
         share(red_mer, ra_send, ra_recv, i, mer, at_mer(lax.rem(mer + i, n_mer))).start()
     for i in range(1, n_mer):
@@ -327,45 +403,10 @@
     total = red_mode[0]
     for i in range(1, n_mode):
         total = total + red_mode[i]
-    dof = float(modes * points * n_mer * width)
-    total = jnp.sum(total, axis=1, keepdims=True) / dof
-    one = [total[n : n + 1, :] for n in range(n_inner + len(pairs) + len(cross))]
-    c_re, c_im = one[0:krylov], one[krylov : 2 * krylov]
-    square = one[2 * krylov]
-    for j in range(krylov):
-        square = square - 2.0 * (c_re[j] * c_re[j] + c_im[j] * c_im[j])
-    for n, (i, j) in enumerate(pairs):
-        both = c_re[i] * c_re[j] + c_im[i] * c_im[j]
-        square = square + (1.0 if i == j else 2.0) * both * one[n_inner + n]
-    for n, (i, j) in enumerate(cross):
-        both = c_re[i] * c_im[j] - c_im[i] * c_re[j]
-        square = square - 2.0 * both * one[n_inner + len(pairs) + n]
-    size = jnp.sqrt(jnp.maximum(square, 0.0) + epsilon)
-    norm[...] = size
-    lane = lax.broadcasted_iota(jnp.int32, coef.shape, 1)
-    side = lax.broadcasted_iota(jnp.int32, coef.shape, 0)
-    table = jnp.zeros(coef.shape, F32)
-    for j in range(krylov):
-        table = jnp.where(lane == j, jnp.where(side == 0, c_re[j], c_im[j]), table)
-    coef[...] = table
-
-    scale = 1.0 / size
-    scaled_re = [jnp.broadcast_to(x * scale, (8, width)) for x in c_re]
-    scaled_im = [jnp.broadcast_to(x * scale, (8, width)) for x in c_im]
-    scale = jnp.broadcast_to(scale, (8, width))
+    lane = lax.broadcasted_iota(jnp.int32, (1, 128), 1)
+    stats[...] = jnp.where(lane == 127, count.astype(F32), total)
     for s in range(slots):
-        live = s < count
-        for t in range(tiles):
-            z = slice(t * 8, (t + 1) * 8)
-            new_re = loc[0, s, z, :] * scale
-            new_im = loc[1, s, z, :] * scale
-            for j in range(krylov):
-                src = cur if j == krylov - 1 else bas.at[j]
-                re, im = src[0, s, z, :], src[1, s, z, :]
-                new_re = new_re - (scaled_re[j] * re - scaled_im[j] * im)
-                new_im = new_im - (scaled_re[j] * im + scaled_im[j] * re)
-            out[0, s, z, :] = jnp.where(live, new_re, 0.0)
-            out[1, s, z, :] = jnp.where(live, new_im, 0.0)
+        pltpu.make_async_copy(loc.at[:, s], w_out.at[:, s], w_sem.at[s]).wait()
 
     for there, copy in ((has_next, to_next), (has_prev, to_prev), (has_right, to_right), (has_left, to_left)):
 
@@ -393,18 +434,13 @@
     hbm = pl.BlockSpec(memory_space=pl.ANY)
     vmem = pl.BlockSpec(memory_space=pltpu.VMEM)
     dma = pltpu.SemaphoreType.DMA
-    new_vector, coeffs, norm = pl.pallas_call(
+    w, stats = pl.pallas_call(
         functools.partial(kernel, n_mode, n_mer, modes),
-        out_shape=[
-            jax.ShapeDtypeStruct(field, F32),
-            jax.ShapeDtypeStruct((2, krylov), F32),
-            jax.ShapeDtypeStruct((1, 1), F32),
-        ],
+        out_shape=[jax.ShapeDtypeStruct(field, F32), jax.ShapeDtypeStruct((1, 128), F32)],
         in_specs=[smem, smem] + [hbm] * 6,
-        out_specs=[vmem] * 3,
+        out_specs=[hbm, vmem],
         scratch_shapes=[
             pltpu.VMEM(field, F32),
-            pltpu.VMEM((2, slots + 4, points, width), F32),
             pltpu.VMEM((krylov - 1,) + field, F32),
             pltpu.VMEM(radial.shape, F32),
             pltpu.VMEM(axial.shape, F32),
@@ -426,9 +462,10 @@
             pltpu.VMEM(field, F32),
             pltpu.VMEM((n_mer, 2) + ends, F32),
             pltpu.VMEM((sums, 128), F32),
-            pltpu.VMEM((n_mer, sums, 128), F32),
-            pltpu.VMEM((n_mode, sums, 128), F32),
-            dma((8,)),
+            pltpu.VMEM((n_mer, 1, 128), F32),
+            pltpu.VMEM((n_mode, 1, 128), F32),
+            dma((7,)),
+            dma((slots,)),
             dma((4,)),
             dma((4,)),
             dma((n_mer,)),
@@ -442,6 +479,25 @@
             collective_id=0, has_side_effects=True, vmem_limit_bytes=60 * 1024 * 1024
         ),
     )(mode_cost, shift, iface_index[None, :], basis, radial, axial, flow_coupling, swirl)
+    new_vector, coeffs, norm = pl.pallas_call(
+        functools.partial(finish, float(modes * points * n_mer * width)),
+        out_shape=[
+            jax.ShapeDtypeStruct(field, F32),
+            jax.ShapeDtypeStruct((2, krylov), F32),
+            jax.ShapeDtypeStruct((1, 1), F32),
+        ],
+        in_specs=[hbm, hbm, vmem],
+        out_specs=[hbm, vmem, vmem],
+        scratch_shapes=[
+            pltpu.VMEM(basis.shape, F32),
+            pltpu.VMEM(field, F32),
+            pltpu.VMEM(field, F32),
+            dma((2,)),
+            dma((2,)),
+            dma((2,)),
+        ],
+        compiler_params=pltpu.CompilerParams(vmem_limit_bytes=60 * 1024 * 1024),
+    )(basis, w, stats)
     return new_vector, coeffs, norm.reshape(())
 
 

time: 32.1 us -> 29.8 us (0.928)
  local copies, waits for them, and re-layouts: 3.08 us -> 0 us
  Pallas kernels: 26.4 us -> 28.9 us
  between operations: 2.41 us -> 0.64 us
    pallas_call x0 -> x1, Pallas kernels: none -> 3.81 us  [body(): pl.pallas_call(functools.partial(finish, float(modes * points * n_mer * w...]
    unnamed x2 -> x0, local copies, waits for them, and re-layouts: 3.08 us -> none
    pallas_call x1, Pallas kernels: 26.4 us -> 25.1 us  [body(): pl.pallas_call(functools.partial(kernel, n_mode, n_mer, modes), out_shape...]
where the time goes in v2:
time: 29.8 us; the launch traced here: 29.6 us
  Pallas kernels  28.9 us (97%)
  between operations  0.64 us (2%)
    pallas_call x1, Pallas kernels, body(): pl.pallas_call(functools.partial(kernel, n_mode, n_mer, modes), out_shape...  25.1 us
    pallas_call x1, Pallas kernels, body(): pl.pallas_call(functools.partial(finish, float(modes * points * n_mer * w...  3.81 us

profile of v2, /device:TPU:0, one launch (start us, length us, event | category | flops | bytes accessed | tf_op | source)
XLA Modules:
  0.0 29.6 jit_solution(6195569443943905498)
XLA Ops:
  0.6 25.1 %shard_map.103 = (f32[2,8,32,256]{3,2,1,0:T(8,128)}, f32[1,128]{1,0:T(1,128)}) custom-call(s32[32]{0:T(128)} %cost.1, f32[2]{0:T(128)} %shift.1, s32[1,128]{1,0:T(1,128)} %bitcast.2, f32[4,2,8,32,256]{4,3,2,1,0:T(8,128)} %basis.3, f32[2,256,256]{2,1,0:T(8,128)} %radial.1, f32[2,32,32]{2,1,0:T(8,128)} %axial.1, f32[4,32,256]{2,1,0:T(8,128)} %flow.1, ...), custom_call_target="tpu_custom_call" | custom-call | tf_op jit(solution)/shard_map/pallas_call | solution.py:437
  25.8 3.8 %shard_map.104 = (f32[2,8,32,256]{3,2,1,0:T(8,128)}, f32[2,4]{1,0:T(2,128)}, f32[1,1]{1,0:T(1,128)}) custom-call(f32[4,2,8,32,256]{4,3,2,1,0:T(8,128)} %basis.3, f32[2,8,32,256]{3,2,1,0:T(8,128)} %get-tuple-element.8.w_in, f32[1,128]{1,0:T(1,128)} %get-tuple-element.9.stats), custom_call_target="tpu_custom_call" | custom-call | tf_op jit(solution)/shard_map/pallas_call | solution.py:482

commit v3 on v2

--- a/solution.py
+++ b/solution.py
@@ -51,10 +51,9 @@
     cross = [(i, j) for i in range(krylov) for j in range(i + 1, krylov)]
     n_inner = 2 * krylov + 1
     sums = n_inner + len(pairs) + len(cross)
-    half = slots // 2
     ins, outs = [], []
-    for n in range(2):
-        at = pl.ds(n * half, half)
+    for n in range(slots):
+        at = pl.ds(n, 1)
         ins.append(pltpu.make_async_copy(basis.at[:, :, at], bas.at[:, :, at], in_sem.at[n]))
         ins.append(pltpu.make_async_copy(w_in.at[:, at], w.at[:, at], w_sem.at[n]))
         outs.append(pltpu.make_async_copy(fresh.at[:, at], out.at[:, at], out_sem.at[n]))
@@ -88,9 +87,8 @@
     scale = jnp.broadcast_to(scale, (8, width))
     live_to = jnp.broadcast_to(count, (8, width))
     for s in range(slots):
-        if s % half == 0:
-            ins[s // half * 2].wait()
-            ins[s // half * 2 + 1].wait()
+        ins[2 * s].wait()
+        ins[2 * s + 1].wait()
         live = live_to > s
         for t in range(tiles):
             z = slice(t * 8, (t + 1) * 8)
@@ -102,8 +100,7 @@
                 new_im = new_im - (scaled_re[j] * im + scaled_im[j] * re)
             fresh[0, s, z, :] = jnp.where(live, new_re, 0.0)
             fresh[1, s, z, :] = jnp.where(live, new_im, 0.0)
-        if s % half == half - 1:
-            outs[s // half].start()
+        outs[s].start()
     for copy in outs:
         copy.wait()
 
@@ -145,8 +142,7 @@
         pltpu.make_async_copy(swirl, swl, local_sem.at[5]),
         pltpu.make_async_copy(basis.at[0 : krylov - 1], bas, local_sem.at[6]),
     ]
-    for load in loads:
-        load.start()
+    loads[0].start()
 
     least = mode * QUOTA
 
@@ -165,9 +161,6 @@
     for c in range(2):
         for i in range(2):
             stage[c, i] = cur[c, ending + i]
-        for s in range(slots):
-            first[c, s : s + 1, :] = cur[c, s, 0:1, :]
-            last[c, s : s + 1, :] = cur[c, s, points - 1 : points, :]
 
     def halo(which, src, dst, device):
         return pltpu.make_async_remote_copy(
@@ -182,7 +175,19 @@
     has_next, has_prev = mode < n_mode - 1, mode > 0
     has_right, has_left = mer < n_mer - 1, mer > 0
     pl.semaphore_wait(barrier, n_mer - 1 + n_mode - 1)
-    for there, copy in ((has_next, to_next), (has_prev, to_prev), (has_right, to_right), (has_left, to_left)):
+    for there, copy in ((has_next, to_next), (has_prev, to_prev)):
+
+        @pl.when(there)
+        def _(copy=copy):
+            copy.start()
+
+    for load in loads[1:]:
+        load.start()
+    for c in range(2):
+        for s in range(slots):
+            first[c, s : s + 1, :] = cur[c, s, 0:1, :]
+            last[c, s : s + 1, :] = cur[c, s, points - 1 : points, :]
+    for there, copy in ((has_right, to_right), (has_left, to_left)):
 
         @pl.when(there)
         def _(copy=copy):
@@ -492,9 +497,9 @@
             pltpu.VMEM(basis.shape, F32),
             pltpu.VMEM(field, F32),
             pltpu.VMEM(field, F32),
-            dma((2,)),
-            dma((2,)),
-            dma((2,)),
+            dma((slots,)),
+            dma((slots,)),
+            dma((slots,)),
         ],
         compiler_params=pltpu.CompilerParams(vmem_limit_bytes=60 * 1024 * 1024),
     )(basis, w, stats)

time: 29.8 us -> 29.8 us (level)
  no operation moved by 1% of the time
where the time goes in v3:
time: 29.8 us; the launch traced here: 29.6 us
  Pallas kernels  28.9 us (97%)
  between operations  0.64 us (2%)
    pallas_call x1, Pallas kernels, body(): pl.pallas_call(functools.partial(kernel, n_mode, n_mer, modes), out_shape...  25.1 us
    pallas_call x1, Pallas kernels, body(): pl.pallas_call(functools.partial(finish, float(modes * points * n_mer * w...  3.79 us

profile of v3, /device:TPU:0, one launch (start us, length us, event | category | flops | bytes accessed | tf_op | source)
XLA Modules:
  0.0 29.6 jit_solution(2036919340456627660)
XLA Ops:
  0.6 25.1 %shard_map.103 = (f32[2,8,32,256]{3,2,1,0:T(8,128)}, f32[1,128]{1,0:T(1,128)}) custom-call(s32[32]{0:T(128)} %cost.1, f32[2]{0:T(128)} %shift.1, s32[1,128]{1,0:T(1,128)} %bitcast.2, f32[4,2,8,32,256]{4,3,2,1,0:T(8,128)} %basis.3, f32[2,256,256]{2,1,0:T(8,128)} %radial.1, f32[2,32,32]{2,1,0:T(8,128)} %axial.1, f32[4,32,256]{2,1,0:T(8,128)} %flow.1, ...), custom_call_target="tpu_custom_call" | custom-call | tf_op jit(solution)/shard_map/pallas_call | solution.py:442
  25.8 3.8 %shard_map.104 = (f32[2,8,32,256]{3,2,1,0:T(8,128)}, f32[2,4]{1,0:T(2,128)}, f32[1,1]{1,0:T(1,128)}) custom-call(f32[4,2,8,32,256]{4,3,2,1,0:T(8,128)} %basis.3, f32[2,8,32,256]{3,2,1,0:T(8,128)} %get-tuple-element.8.w_in, f32[1,128]{1,0:T(1,128)} %get-tuple-element.9.stats), custom_call_target="tpu_custom_call" | custom-call | tf_op jit(solution)/shard_map/pallas_call | solution.py:487

commit v4 on v3

--- a/solution.py
+++ b/solution.py
@@ -272,6 +272,46 @@
                     acc = acc + jnp.where(sub8 == 7, penalty * mhi[c, s : s + 1, :], 0.0)
                 img[c, s, z, :] = acc
 
+    @pl.when(has_prev)
+    def _():
+        to_next.wait_recv()
+        for c in range(2):
+            img[c, 0] = img[c, 0] + (flw[0] * low[c, 0] + flw[1] * low[c, 1])
+            img[c, 1] = img[c, 1] + flw[0] * low[c, 1]
+
+    @pl.when(has_next)
+    def _():
+        to_prev.wait_recv()
+        for c in range(2):
+            one_up = jnp.where(upto < modes, up[c, 0], 0.0)
+            two_up = jnp.where(upto + 1 < modes, up[c, 1], 0.0)
+            on_last = flw[2] * one_up + flw[3] * two_up
+            on_second = flw[3] * one_up
+            for s in range(slots):
+                term = jnp.where(s == count - 1, on_last, jnp.where(s == count - 2, on_second, 0.0))
+                img[c, s] = img[c, s] + term
+
+    inner = []
+    for c in range(2):
+        xh, xl = split(img[c].reshape(rows, width))
+        y = mm(dh[1], xh) + mm(dl[1], xh) + mm(dh[1], xl)
+        ends = split(y[rows : rows + 2 * slots])
+        both = mmt(ends[0], rh[1]) + mmt(ends[1], rh[1]) + mmt(ends[0], rl[1])
+        trs[mer, 0, c] = both[0:slots]
+        trs[mer, 1, c] = both[slots : 2 * slots]
+        inner.append(y[0:rows])
+
+    def trace(i, slot, to):
+        return pltpu.make_async_remote_copy(
+            src_ref=trs.at[slot], dst_ref=trs.at[slot], send_sem=tr_send.at[i], recv_sem=tr_recv.at[i],
+            device_id=at_mer(to), device_id_type=mesh_id,
+        )
+
+    for i in range(1, n_mer):
+        trace(i, mer, lax.rem(mer + i, n_mer)).start()
+    for c in range(2):
+        yh, yl = split(inner[c])
+        loc[c] = (mmt(yh, rh[1]) + mmt(yl, rh[1]) + mmt(yh, rl[1])).reshape(slots, points, width)
     loads[6].wait()
     pairs = [(i, j) for i in range(krylov) for j in range(i, krylov)]
     cross = [(i, j) for i in range(krylov) for j in range(i + 1, krylov)]
@@ -304,46 +344,6 @@
     for n, x in enumerate(grams):
         part[n_inner + n : n_inner + n + 1, :] = fold(x)
 
-    @pl.when(has_prev)
-    def _():
-        to_next.wait_recv()
-        for c in range(2):
-            img[c, 0] = img[c, 0] + (flw[0] * low[c, 0] + flw[1] * low[c, 1])
-            img[c, 1] = img[c, 1] + flw[0] * low[c, 1]
-
-    @pl.when(has_next)
-    def _():
-        to_prev.wait_recv()
-        for c in range(2):
-            one_up = jnp.where(upto < modes, up[c, 0], 0.0)
-            two_up = jnp.where(upto + 1 < modes, up[c, 1], 0.0)
-            on_last = flw[2] * one_up + flw[3] * two_up
-            on_second = flw[3] * one_up
-            for s in range(slots):
-                term = jnp.where(s == count - 1, on_last, jnp.where(s == count - 2, on_second, 0.0))
-                img[c, s] = img[c, s] + term
-
-    inner = []
-    for c in range(2):
-        xh, xl = split(img[c].reshape(rows, width))
-        y = mm(dh[1], xh) + mm(dl[1], xh) + mm(dh[1], xl)
-        ends = split(y[rows : rows + 2 * slots])
-        both = mmt(ends[0], rh[1]) + mmt(ends[1], rh[1]) + mmt(ends[0], rl[1])
-        trs[mer, 0, c] = both[0:slots]
-        trs[mer, 1, c] = both[slots : 2 * slots]
-        inner.append(y[0:rows])
-
-    def trace(i, slot, to):
-        return pltpu.make_async_remote_copy(
-            src_ref=trs.at[slot], dst_ref=trs.at[slot], send_sem=tr_send.at[i], recv_sem=tr_recv.at[i],
-            device_id=at_mer(to), device_id_type=mesh_id,
-        )
-
-    for i in range(1, n_mer):
-        trace(i, mer, lax.rem(mer + i, n_mer)).start()
-    for c in range(2):
-        yh, yl = split(inner[c])
-        loc[c] = (mmt(yh, rh[1]) + mmt(yl, rh[1]) + mmt(yh, rl[1])).reshape(slots, points, width)
     for i in range(1, n_mer):
         trace(i, lax.rem(mer + n_mer - i, n_mer), mer).wait_recv()
 

time: 29.8 us -> 29.8 us (level)
  no operation moved by 1% of the time
where the time goes in v4:
time: 29.8 us; the launch traced here: 29.6 us
  Pallas kernels  28.9 us (97%)
  between operations  0.64 us (2%)
    pallas_call x1, Pallas kernels, body(): pl.pallas_call(functools.partial(kernel, n_mode, n_mer, modes), out_shape...  25.1 us
    pallas_call x1, Pallas kernels, body(): pl.pallas_call(functools.partial(finish, float(modes * points * n_mer * w...  3.79 us

profile of v4, /device:TPU:0, one launch (start us, length us, event | category | flops | bytes accessed | tf_op | source)
XLA Modules:
  0.0 29.6 jit_solution(6731100723292382832)
XLA Ops:
  0.6 25.1 %shard_map.103 = (f32[2,8,32,256]{3,2,1,0:T(8,128)}, f32[1,128]{1,0:T(1,128)}) custom-call(s32[32]{0:T(128)} %cost.1, f32[2]{0:T(128)} %shift.1, s32[1,128]{1,0:T(1,128)} %bitcast.2, f32[4,2,8,32,256]{4,3,2,1,0:T(8,128)} %basis.3, f32[2,256,256]{2,1,0:T(8,128)} %radial.1, f32[2,32,32]{2,1,0:T(8,128)} %axial.1, f32[4,32,256]{2,1,0:T(8,128)} %flow.1, ...), custom_call_target="tpu_custom_call" | custom-call | tf_op jit(solution)/shard_map/pallas_call | solution.py:442
  25.8 3.8 %shard_map.104 = (f32[2,8,32,256]{3,2,1,0:T(8,128)}, f32[2,4]{1,0:T(2,128)}, f32[1,1]{1,0:T(1,128)}) custom-call(f32[4,2,8,32,256]{4,3,2,1,0:T(8,128)} %basis.3, f32[2,8,32,256]{3,2,1,0:T(8,128)} %get-tuple-element.8.w_in, f32[1,128]{1,0:T(1,128)} %get-tuple-element.9.stats), custom_call_target="tpu_custom_call" | custom-call | tf_op jit(solution)/shard_map/pallas_call | solution.py:487
